TPU v7x, 32 devices: a whole 2x2x4 slice. The times are simulated.
32 devices in a mesh: seq: 8 (over y, x, core), tp: 4 (over z).
Axes of the slice: x: 2, y: 2, z: 4, core: 2. Of those that a mesh axis runs over, the one named last changes fastest.
Arguments:
- query_rows: bfloat16 [1024, 4096], P('seq', 'tp'), may hold values from -6 to 6
- key_rows: bfloat16 [1024, 4096], P('seq', 'tp'), may hold values from -6 to 6
- value_rows: bfloat16 [1024, 4096], P('seq', 'tp'), may hold values from -6 to 6
- short_taps: float32 [3, 4096], P(None, 'tp'), may hold values from -3.5 to 3.5
- decay_rates: float32 [256, 16], P('tp'), may hold values from 0 to 1, as said below
- residues: float32 [256, 16], P('tp'), may hold values from -1 to 1
- skip_gain: float32 [4096], P('tp'), may hold values from -4 to 4
- out_weight: bfloat16 [4096, 4096], P('tp'), may hold values from -0.09375 to 0.09375
Outputs:
- mixed_out: bfloat16 [1024, 4096], P('seq', 'tp')
Inputs may be any that keep to these rules, and one draw needn't show every extreme that they name: `decay_rates`: positive decay rates.
All inputs are finite; a program needn't handle non-finite values.
Results may differ from a plain program's by a relative error of at most 0.0095.
Values may be sent and summed in bfloat16 or wider, within the bound.
A program may use at most 64 MiB of HBM per device.

v0:
```python
import functools

import jax
import jax.numpy as jnp
from jax import lax
from jax.experimental import pallas as pl
from jax.experimental.pallas import tpu as pltpu
from jax.sharding import PartitionSpec as P

MESH = pl.DeviceIdType.MESH
F32 = jnp.float32
LANES = 128


def kernel(
    n_seq, n_tp, pieces,
    q_ref, k_ref, v_ref, taps_ref, rates_ref, res_ref, skip_ref, w_hbm,
    out_ref,
    w_vmem, ext_ref, qf_ref, x3_ref, y3_ref, a3_ref, ar3_ref, r3_ref, s3_ref,
    halo_out, halo_in, state_ref, gathered, carries, carry_in, gated_ref,
    acc_ref, from_left, from_right,
    w_sem, halo_sem, st_send, st_recv, ca_send, ca_recv,
    right_send, right_recv, left_send, left_recv,
):
    rows, chans = q_ref.shape
    groups, modes = rates_ref.shape
    subs = chans // LANES
    group_size = chans // groups
    owners = min(n_seq, modes)
    per_owner = modes // owners
    width = w_vmem.shape[2]
    me = lax.axis_index("seq")
    z = lax.axis_index("tp")

    loads = []
    for i in range(n_tp * pieces):
        load = pltpu.make_async_copy(
            w_hbm.at[:, pl.ds(i * width, width)], w_vmem.at[i], w_sem.at[i]
        )
        load.start()
        loads.append(load)

    barrier = pltpu.get_barrier_semaphore()
    for off in range(1, n_seq):
        pl.semaphore_signal(
            barrier, inc=1, device_id={"seq": lax.rem(me + off, n_seq)}, device_id_type=MESH
        )

    @pl.when(z > 0)
    def _():
        pl.semaphore_signal(barrier, inc=1, device_id={"tp": z - 1}, device_id_type=MESH)

    @pl.when(z < n_tp - 1)
    def _():
        pl.semaphore_signal(barrier, inc=1, device_id={"tp": z + 1}, device_id_type=MESH)

    branch_refs = (q_ref, k_ref, v_ref)
    halo_out[...] = jnp.zeros_like(halo_out)
    for b, ref in enumerate(branch_refs):
        tail = ref[rows - 16 : rows, :].astype(F32)
        halo_out[2 * b : 2 * b + 2, :] = tail[14:16]

    edges = jnp.where(z > 0, 1, 0) + jnp.where(z < n_tp - 1, 1, 0)
    pl.semaphore_wait(barrier, n_seq - 1 + edges)

    halo_copy = pltpu.make_async_remote_copy(
        src_ref=halo_out,
        dst_ref=halo_in,
        send_sem=halo_sem.at[0],
        recv_sem=halo_sem.at[1],
        device_id={"seq": lax.rem(me + 1, n_seq)},
        device_id_type=MESH,
    )

    @pl.when(me < n_seq - 1)
    def _():
        halo_copy.start()

    chan_id = lax.broadcasted_iota(jnp.int32, (groups, chans), 1)
    group_id = lax.broadcasted_iota(jnp.int32, (groups, chans), 0)
    onehot = (chan_id // group_size == group_id).astype(F32)
    dims = (((0,), (0,)), ((), ()))
    rate_nat = lax.dot_general(
        rates_ref[...], onehot, dims, precision=lax.Precision.HIGHEST, preferred_element_type=F32
    )
    res_nat = lax.dot_general(
        res_ref[...], onehot, dims, precision=lax.Precision.HIGHEST, preferred_element_type=F32
    )
    for s in range(subs):
        cols = slice(s * LANES, (s + 1) * LANES)
        rate = rate_nat[:, cols]
        a3_ref[:, s, :] = jnp.exp(-rate)
        ar3_ref[:, s, :] = jnp.exp(-rate * float(rows))
        r3_ref[:, s, :] = res_nat[:, cols]
        s3_ref[s : s + 1, :] = skip_ref[0:1, cols]

    for b, ref in enumerate(branch_refs):
        ext_ref[b, 8 : 8 + rows, :] = ref[...].astype(F32)

    @pl.when(me == 0)
    def _():
        halo_in[...] = jnp.zeros_like(halo_in)

    @pl.when(me > 0)
    def _():
        halo_copy.wait_recv()

    for b in range(3):
        ext_ref[b, 6:8, :] = halo_in[2 * b : 2 * b + 2, :]

    def feature(b, cols):
        return (
            taps_ref[0:1, cols] * ext_ref[b, 8 : 8 + rows, cols]
            + taps_ref[1:2, cols] * ext_ref[b, 7 : 7 + rows, cols]
            + taps_ref[2:3, cols] * ext_ref[b, 6 : 6 + rows, cols]
        )

    for s in range(subs):
        cols = slice(s * LANES, (s + 1) * LANES)
        x3_ref[:, s, :] = feature(1, cols) * feature(2, cols)

    decays = [a3_ref[r] for r in range(modes)]

    def state_step(t, hs):
        x = x3_ref[t]
        return tuple(decays[r] * hs[r] + x for r in range(modes))

    zero = jnp.zeros((subs, LANES), F32)
    hs = lax.fori_loop(0, rows, state_step, (zero,) * modes, unroll=4)
    for r in range(modes):
        state_ref[r] = hs[r]

    def state_copy(off):
        to = lax.rem(me + off, n_seq)
        return pltpu.make_async_remote_copy(
            src_ref=state_ref.at[pl.ds(to * per_owner, per_owner)],
            dst_ref=gathered.at[me],
            send_sem=st_send.at[off],
            recv_sem=st_recv.at[off],
            device_id={"seq": to},
            device_id_type=MESH,
        ), to

    def carry_copy(off):
        to = lax.rem(me + off, n_seq)
        return pltpu.make_async_remote_copy(
            src_ref=carries.at[to],
            dst_ref=carry_in.at[pl.ds(me * per_owner, per_owner)],
            send_sem=ca_send.at[off],
            recv_sem=ca_recv.at[off],
            device_id={"seq": to},
            device_id_type=MESH,
        ), to

    def when_owner(index, act):
        if owners == n_seq:
            act()
        else:
            pl.when(index < owners)(act)

    for off in range(1, n_seq):
        copy, to = state_copy(off)
        when_owner(to, copy.start)

    for s in range(subs):
        cols = slice(s * LANES, (s + 1) * LANES)
        qf_ref[:, cols] = feature(0, cols)

    weights = [r3_ref[r] for r in range(modes)]
    skip = s3_ref[...]

    def local_step(t, hs):
        x = x3_ref[t]
        y = skip * x
        out = []
        for r in range(modes):
            h = decays[r] * hs[r] + x
            y = y + weights[r] * h
            out.append(h)
        y3_ref[t] = y
        return tuple(out)

    lax.fori_loop(0, rows, local_step, (zero,) * modes, unroll=2)

    def own_modes():
        mine = pl.ds(me * per_owner, per_owner)
        gathered[me] = state_ref[mine]
        for off in range(1, n_seq):
            state_copy(off)[0].wait_recv()
        block_decay = ar3_ref[mine]
        carry = jnp.zeros((per_owner, subs, LANES), F32)
        for j in range(n_seq):
            carries[j] = carry
            carry = block_decay * carry + gathered[j]
        for off in range(1, n_seq):
            carry_copy(off)[0].start()
        carry_in[mine] = carries[me]

    when_owner(me, own_modes)
    for off in range(1, n_seq):
        sender = lax.rem(me - off + n_seq, n_seq)
        when_owner(sender, carry_copy(off)[0].wait_recv)

    def carry_step(t, gs):
        y = y3_ref[t]
        for r in range(modes):
            y = y + gs[r]
        y3_ref[t] = y
        return tuple(decays[r] * gs[r] for r in range(modes))

    gs = tuple(weights[r] * (decays[r] * carry_in[r]) for r in range(modes))
    lax.fori_loop(0, rows, carry_step, gs, unroll=4)

    for s in range(subs):
        cols = slice(s * LANES, (s + 1) * LANES)
        gated_ref[:, cols] = (qf_ref[:, cols] * y3_ref[:, s, :]).astype(jnp.bfloat16)

    for load in loads:
        load.wait()

    def product(i):
        return jnp.dot(gated_ref[...], w_vmem[i], preferred_element_type=F32)

    def right_copy(i):
        return pltpu.make_async_remote_copy(
            src_ref=acc_ref.at[i], dst_ref=from_left.at[i],
            send_sem=right_send.at[i], recv_sem=right_recv.at[i],
            device_id={"tp": jnp.minimum(z + 1, n_tp - 1)}, device_id_type=MESH,
        )

    def left_copy(i):
        return pltpu.make_async_remote_copy(
            src_ref=acc_ref.at[i], dst_ref=from_right.at[i],
            send_sem=left_send.at[i], recv_sem=left_recv.at[i],
            device_id={"tp": jnp.maximum(z - 1, 0)}, device_id_type=MESH,
        )

    def chain_step(step, _):
        block, piece = step // pieces, step % pieces
        right_block = n_tp - 1 - block
        left_block = block

        @pl.when(right_block > z)
        def _():
            i = right_block * pieces + piece
            part = product(i)

            @pl.when(z == 0)
            def _():
                acc_ref[i] = part.astype(jnp.bfloat16)

            @pl.when(z > 0)
            def _():
                right_copy(i).wait_recv()
                acc_ref[i] = (part + from_left[i].astype(F32)).astype(jnp.bfloat16)

            right_copy(i).start()

        @pl.when(left_block < z)
        def _():
            i = left_block * pieces + piece
            part = product(i)

            @pl.when(z == n_tp - 1)
            def _():
                acc_ref[i] = part.astype(jnp.bfloat16)

            @pl.when(z < n_tp - 1)
            def _():
                left_copy(i).wait_recv()
                acc_ref[i] = (part + from_right[i].astype(F32)).astype(jnp.bfloat16)

            left_copy(i).start()

        return 0

    lax.fori_loop(0, (n_tp - 1) * pieces, chain_step, 0)

    for piece in range(pieces):
        i = z * pieces + piece
        cols = slice(piece * width, (piece + 1) * width)
        total = product(i)
        acc_ref[i] = total.astype(jnp.bfloat16)

        @pl.when(z > 0)
        def _():
            right_copy(i).wait_recv()

        @pl.when(z < n_tp - 1)
        def _():
            left_copy(i).wait_recv()

        @pl.when(z == 0)
        def _():
            out_ref[:, cols] = (total + from_right[i].astype(F32)).astype(jnp.bfloat16)

        @pl.when(z == n_tp - 1)
        def _():
            out_ref[:, cols] = (total + from_left[i].astype(F32)).astype(jnp.bfloat16)

        @pl.when(jnp.logical_and(z > 0, z < n_tp - 1))
        def _():
            out_ref[:, cols] = (
                total + from_left[i].astype(F32) + from_right[i].astype(F32)
            ).astype(jnp.bfloat16)

    @pl.when(me < n_seq - 1)
    def _():
        halo_copy.wait_send()

    for off in range(1, n_seq):
        copy, to = state_copy(off)
        when_owner(to, copy.wait_send)
        when_owner(me, carry_copy(off)[0].wait_send)

    def drain(step, _):
        block, piece = step // pieces, step % pieces
        i = block * pieces + piece

        @pl.when(block > z)
        def _():
            right_copy(i).wait_send()

        @pl.when(block < z)
        def _():
            left_copy(i).wait_send()

        return 0

    lax.fori_loop(0, n_tp * pieces, drain, 0)


def body(n_seq, n_tp, q, k, v, taps, rates, res, skip, w):
    rows, chans = q.shape
    groups, modes = rates.shape
    subs = chans // LANES
    owners = min(n_seq, modes)
    per_owner = modes // owners
    dout = w.shape[1]
    block = dout // n_tp
    width = min(256, block)
    pieces = block // width
    total = n_tp * pieces
    vmem = pl.BlockSpec(memory_space=pltpu.VMEM)
    dma = pltpu.SemaphoreType.DMA
    return pl.pallas_call(
        functools.partial(kernel, n_seq, n_tp, pieces),
        out_shape=jax.ShapeDtypeStruct((rows, block), jnp.bfloat16),
        in_specs=[vmem] * 7 + [pl.BlockSpec(memory_space=pl.ANY)],
        out_specs=vmem,
        scratch_shapes=[
            pltpu.VMEM((total, chans, width), jnp.bfloat16),
            pltpu.VMEM((3, rows + 8, chans), F32),
            pltpu.VMEM((rows, chans), F32),
            pltpu.VMEM((rows, subs, LANES), F32),
            pltpu.VMEM((rows, subs, LANES), F32),
            pltpu.VMEM((modes, subs, LANES), F32),
            pltpu.VMEM((modes, subs, LANES), F32),
            pltpu.VMEM((modes, subs, LANES), F32),
            pltpu.VMEM((subs, LANES), F32),
            pltpu.VMEM((8, chans), F32),
            pltpu.VMEM((8, chans), F32),
            pltpu.VMEM((modes, subs, LANES), F32),
            pltpu.VMEM((n_seq, per_owner, subs, LANES), F32),
            pltpu.VMEM((n_seq, per_owner, subs, LANES), F32),
            pltpu.VMEM((modes, subs, LANES), F32),
            pltpu.VMEM((rows, chans), jnp.bfloat16),
            pltpu.VMEM((total, rows, width), jnp.bfloat16),
            pltpu.VMEM((total, rows, width), jnp.bfloat16),
            pltpu.VMEM((total, rows, width), jnp.bfloat16),
            dma((total,)),
            dma((2,)),
            dma((n_seq,)), dma((n_seq,)), dma((n_seq,)), dma((n_seq,)),
            dma((total,)), dma((total,)), dma((total,)), dma((total,)),
        ],
        compiler_params=pltpu.CompilerParams(
            collective_id=0, has_side_effects=True, vmem_limit_bytes=48 * 1024 * 1024
        ),
    )(q, k, v, taps, rates, res, skip.reshape(1, chans), w)


def solution(mesh):
    placed = (
        P("seq", "tp"),
        P("seq", "tp"),
        P("seq", "tp"),
        P(None, "tp"),
        P("tp", None),
        P("tp", None),
        P("tp"),
        P("tp", None),
    )
    return jax.shard_map(
        functools.partial(body, mesh.shape["seq"], mesh.shape["tp"]),
        mesh=mesh, in_specs=placed, out_specs=P("seq", "tp"), check_vma=False,
    )
```

profile of v0, /device:TPU:0, one launch (start us, length us, event | category | flops | bytes accessed | tf_op | source)
XLA Modules:
  0.0 58.9 jit_solution(7197585700749269606)
XLA Ops:
  0.0 0.8 %copy.9.rates_ref = f32[64,16]{1,0:T(8,128)S(1)} copy(f32[64,16]{0,1:T(8,128)} %param.12) | data formatting | bytes 8192 | tf_op args[4]
  0.8 0.8 %copy.10.res_ref = f32[64,16]{1,0:T(8,128)S(1)} copy(f32[64,16]{0,1:T(8,128)} %param.13) | data formatting | bytes 8192 | tf_op args[5]
  1.6 0.0 copy-start
  1.6 0.9 %copy-done = bf16[128,1024]{1,0:T(8,128)(2,1)S(1)} copy-done((bf16[128,1024]{1,0:T(8,128)(2,1)S(1)}, bf16[128,1024]{1,0:T(8,128)(2,1)}, u32[]{:S(2)}) %copy-start) | copy-done | bytes 262168
  2.5 0.0 copy-start.1
  2.5 0.9 %copy-done.1 = bf16[128,1024]{1,0:T(8,128)(2,1)S(1)} copy-done((bf16[128,1024]{1,0:T(8,128)(2,1)S(1)}, bf16[128,1024]{1,0:T(8,128)(2,1)}, u32[]{:S(2)}) %copy-start.1) | copy-done | bytes 262168
  3.5 0.0 copy-start.2
  3.5 0.9 %copy-done.2 = bf16[128,1024]{1,0:T(8,128)(2,1)S(1)} copy-done((bf16[128,1024]{1,0:T(8,128)(2,1)S(1)}, bf16[128,1024]{1,0:T(8,128)(2,1)}, u32[]{:S(2)}) %copy-start.2) | copy-done | bytes 262168
  4.4 0.0 copy-start.3
  4.4 0.7 %copy-done.3 = f32[3,1024]{1,0:T(4,128)S(1)} copy-done((f32[3,1024]{1,0:T(4,128)S(1)}, f32[3,1024]{1,0:T(4,128)}, u32[]{:S(2)}) %copy-start.3) | copy-done | bytes 12312
  5.1 0.0 copy-start.4
  5.1 0.7 %copy-done.4 = f32[1024]{0:T(1024)S(1)} copy-done((f32[1024]{0:T(1024)S(1)}, f32[1024]{0:T(1024)}, u32[]{:S(2)}) %copy-start.4) | copy-done | bytes 4120
  5.8 52.4 %shard_map.82 = bf16[128,1024]{1,0:T(8,128)(2,1)S(1)} custom-call(bf16[128,1024]{1,0:T(8,128)(2,1)S(1)} %copy-done, bf16[128,1024]{1,0:T(8,128)(2,1)S(1)} %copy-done.1, bf16[128,1024]{1,0:T(8,128)(2,1)S(1)} %copy-done.2, f32[3,1024]{1,0:T(4,128)S(1)} %copy-done.3, f32[64,16]{1,0:T(8,128)S(1)} %copy.9.rates_ref, f32[64,16]{1,0:T(8,128)S(1)} %copy.10.res_ref, ...), custom_call_target="tpu_custom_call" | custom-call | tf_op jit(solution)/shard_map/pallas_call | solution.py:346
  58.2 0.7 %copy.12 = bf16[128,1024]{1,0:T(8,128)(2,1)} copy(bf16[128,1024]{1,0:T(8,128)(2,1)S(1)} %shard_map.82) | data formatting | bytes 524288
Async XLA Ops:
  1.6 1.0 %copy-start = (bf16[128,1024]{1,0:T(8,128)(2,1)S(1)}, bf16[128,1024]{1,0:T(8,128)(2,1)}, u32[]{:S(2)}) copy-start(bf16[128,1024]{1,0:T(8,128)(2,1)} %q_ref.1) | copy-start | bytes 786436
  2.5 0.9 %copy-start.1 = (bf16[128,1024]{1,0:T(8,128)(2,1)S(1)}, bf16[128,1024]{1,0:T(8,128)(2,1)}, u32[]{:S(2)}) copy-start(bf16[128,1024]{1,0:T(8,128)(2,1)} %k_ref.1) | copy-start | bytes 786436
  3.5 0.9 %copy-start.2 = (bf16[128,1024]{1,0:T(8,128)(2,1)S(1)}, bf16[128,1024]{1,0:T(8,128)(2,1)}, u32[]{:S(2)}) copy-start(bf16[128,1024]{1,0:T(8,128)(2,1)} %v_ref.1) | copy-start | bytes 786436
  4.4 0.7 %copy-start.3 = (f32[3,1024]{1,0:T(4,128)S(1)}, f32[3,1024]{1,0:T(4,128)}, u32[]{:S(2)}) copy-start(f32[3,1024]{1,0:T(4,128)} %taps_ref.1) | copy-start | bytes 36868
  5.1 0.7 %copy-start.4 = (f32[1024]{0:T(1024)S(1)}, f32[1024]{0:T(1024)}, u32[]{:S(2)}) copy-start(f32[1024]{0:T(1024)} %param.14) | copy-start | bytes 12292
where the time goes:
time: 59.3 us; the launch traced here: 58.9 us
  Pallas kernels  52.4 us (88%)
  local copies, waits for them, and re-layouts  6.52 us (11%)
    pallas_call x1, Pallas kernels, body(): pl.pallas_call(functools.partial(kernel, n_seq, n_tp, pieces), out_shape=...  52.4 us
    unnamed x13, local copies, waits for them, and re-layouts  6.52 us

commit v1 on v0

--- a/solution.py
+++ b/solution.py
@@ -14,16 +14,17 @@
 
 def kernel(
     n_seq, n_tp, pieces,
-    q_ref, k_ref, v_ref, taps_ref, rates_ref, res_ref, skip_ref, w_hbm,
+    q_hbm, k_hbm, v_hbm, taps_hbm, rates_hbm, res_hbm, skip_hbm, w_hbm,
     out_ref,
-    w_vmem, ext_ref, qf_ref, x3_ref, y3_ref, a3_ref, ar3_ref, r3_ref, s3_ref,
+    qkv_ref, taps_ref, rates_ref, res_ref, skip_ref, w_vmem,
+    ext_ref, qf_ref, x3_ref, y3_ref, a3_ref, ar3_ref, r3_ref, s3_ref,
     halo_out, halo_in, state_ref, gathered, carries, carry_in, gated_ref,
-    acc_ref, from_left, from_right,
-    w_sem, halo_sem, st_send, st_recv, ca_send, ca_recv,
-    right_send, right_recv, left_send, left_recv,
+    acc_ref, from_mate, final_in, acc_own,
+    in_sem, w_sem, halo_sem, st_send, st_recv, ca_send, ca_recv,
+    out_send, mate_recv, final_recv,
 ):
-    rows, chans = q_ref.shape
-    groups, modes = rates_ref.shape
+    rows, chans = q_hbm.shape
+    modes, groups = rates_ref.shape
     subs = chans // LANES
     group_size = chans // groups
     owners = min(n_seq, modes)
@@ -32,36 +33,45 @@
     me = lax.axis_index("seq")
     z = lax.axis_index("tp")
 
-    loads = []
-    for i in range(n_tp * pieces):
-        load = pltpu.make_async_copy(
-            w_hbm.at[:, pl.ds(i * width, width)], w_vmem.at[i], w_sem.at[i]
-        )
-        load.start()
-        loads.append(load)
+    inputs = [
+        pltpu.make_async_copy(src, dst, in_sem.at[i])
+        for i, (src, dst) in enumerate((
+            (q_hbm, qkv_ref.at[0]), (k_hbm, qkv_ref.at[1]), (v_hbm, qkv_ref.at[2]),
+            (rates_hbm, rates_ref), (res_hbm, res_ref),
+            (taps_hbm, taps_ref), (skip_hbm, skip_ref),
+        ))
+    ]
+    for copy in inputs:
+        copy.start()
 
     barrier = pltpu.get_barrier_semaphore()
     for off in range(1, n_seq):
         pl.semaphore_signal(
             barrier, inc=1, device_id={"seq": lax.rem(me + off, n_seq)}, device_id_type=MESH
         )
-
-    @pl.when(z > 0)
-    def _():
-        pl.semaphore_signal(barrier, inc=1, device_id={"tp": z - 1}, device_id_type=MESH)
-
-    @pl.when(z < n_tp - 1)
-    def _():
-        pl.semaphore_signal(barrier, inc=1, device_id={"tp": z + 1}, device_id_type=MESH)
-
-    branch_refs = (q_ref, k_ref, v_ref)
+    for off in range(1, n_tp):
+        pl.semaphore_signal(
+            barrier, inc=1, device_id={"tp": lax.rem(z + off, n_tp)}, device_id_type=MESH
+        )
+
+    loads = [
+        pltpu.make_async_copy(
+            w_hbm.at[:, pl.ds(i * width, width)], w_vmem.at[i], w_sem.at[i]
+        )
+        for i in range(n_tp * pieces)
+    ]
+
     halo_out[...] = jnp.zeros_like(halo_out)
-    for b, ref in enumerate(branch_refs):
-        tail = ref[rows - 16 : rows, :].astype(F32)
+    for b in range(3):
+        inputs[b].wait()
+        tail = qkv_ref[b, rows - 16 : rows, :].astype(F32)
         halo_out[2 * b : 2 * b + 2, :] = tail[14:16]
-
-    edges = jnp.where(z > 0, 1, 0) + jnp.where(z < n_tp - 1, 1, 0)
-    pl.semaphore_wait(barrier, n_seq - 1 + edges)
+    for copy in inputs[3:]:
+        copy.wait()
+    for load in loads:
+        load.start()
+
+    pl.semaphore_wait(barrier, n_seq - 1 + n_tp - 1)
 
     halo_copy = pltpu.make_async_remote_copy(
         src_ref=halo_out,
@@ -79,7 +89,7 @@
     chan_id = lax.broadcasted_iota(jnp.int32, (groups, chans), 1)
     group_id = lax.broadcasted_iota(jnp.int32, (groups, chans), 0)
     onehot = (chan_id // group_size == group_id).astype(F32)
-    dims = (((0,), (0,)), ((), ()))
+    dims = (((1,), (0,)), ((), ()))
     rate_nat = lax.dot_general(
         rates_ref[...], onehot, dims, precision=lax.Precision.HIGHEST, preferred_element_type=F32
     )
@@ -94,8 +104,8 @@
         r3_ref[:, s, :] = res_nat[:, cols]
         s3_ref[s : s + 1, :] = skip_ref[0:1, cols]
 
-    for b, ref in enumerate(branch_refs):
-        ext_ref[b, 8 : 8 + rows, :] = ref[...].astype(F32)
+    for b in range(3):
+        ext_ref[b, 8 : 8 + rows, :] = qkv_ref[b].astype(F32)
 
     @pl.when(me == 0)
     def _():
@@ -221,88 +231,77 @@
     def product(i):
         return jnp.dot(gated_ref[...], w_vmem[i], preferred_element_type=F32)
 
-    def right_copy(i):
+    low = lax.rem(z, 2) == 0
+    pair = z // 2
+    mate = z + 1 - 2 * lax.rem(z, 2)
+
+    def mate_copy(i):
         return pltpu.make_async_remote_copy(
-            src_ref=acc_ref.at[i], dst_ref=from_left.at[i],
-            send_sem=right_send.at[i], recv_sem=right_recv.at[i],
-            device_id={"tp": jnp.minimum(z + 1, n_tp - 1)}, device_id_type=MESH,
-        )
-
-    def left_copy(i):
+            src_ref=acc_ref.at[i], dst_ref=from_mate.at[i],
+            send_sem=out_send.at[i], recv_sem=mate_recv.at[i],
+            device_id={"tp": mate}, device_id_type=MESH,
+        )
+
+    def final_copy(block, piece, sender_pair):
+        i = block * pieces + piece
+        slot = sender_pair * pieces + piece
         return pltpu.make_async_remote_copy(
-            src_ref=acc_ref.at[i], dst_ref=from_right.at[i],
-            send_sem=left_send.at[i], recv_sem=left_recv.at[i],
-            device_id={"tp": jnp.maximum(z - 1, 0)}, device_id_type=MESH,
-        )
-
-    def chain_step(step, _):
-        block, piece = step // pieces, step % pieces
-        right_block = n_tp - 1 - block
-        left_block = block
-
-        @pl.when(right_block > z)
+            src_ref=acc_ref.at[i], dst_ref=final_in.at[slot],
+            send_sem=out_send.at[i], recv_sem=final_recv.at[slot],
+            device_id={"tp": block}, device_id_type=MESH,
+        )
+
+    def relay_step(step, _):
+        turn, piece = step // pieces, step % pieces
+        block = jnp.where(low, n_tp - 1 - turn, turn)
+
+        @pl.when(jnp.where(low, block > z + 1, block < z - 1))
         def _():
-            i = right_block * pieces + piece
+            i = block * pieces + piece
+            acc_ref[i] = product(i).astype(jnp.bfloat16)
+            mate_copy(i).start()
+
+        return 0
+
+    lax.fori_loop(0, n_tp * pieces, relay_step, 0)
+
+    def mate_step(piece, _):
+        i = mate * pieces + piece
+        acc_ref[i] = product(i).astype(jnp.bfloat16)
+        mate_copy(i).start()
+        return 0
+
+    lax.fori_loop(0, pieces, mate_step, 0)
+
+    def pair_step(step, _):
+        turn, piece = step // pieces, step % pieces
+        block = jnp.where(low, turn, n_tp - 1 - turn)
+
+        @pl.when(jnp.where(low, block < z, block > z))
+        def _():
+            i = block * pieces + piece
             part = product(i)
-
-            @pl.when(z == 0)
-            def _():
-                acc_ref[i] = part.astype(jnp.bfloat16)
-
-            @pl.when(z > 0)
-            def _():
-                right_copy(i).wait_recv()
-                acc_ref[i] = (part + from_left[i].astype(F32)).astype(jnp.bfloat16)
-
-            right_copy(i).start()
-
-        @pl.when(left_block < z)
-        def _():
-            i = left_block * pieces + piece
-            part = product(i)
-
-            @pl.when(z == n_tp - 1)
-            def _():
-                acc_ref[i] = part.astype(jnp.bfloat16)
-
-            @pl.when(z < n_tp - 1)
-            def _():
-                left_copy(i).wait_recv()
-                acc_ref[i] = (part + from_right[i].astype(F32)).astype(jnp.bfloat16)
-
-            left_copy(i).start()
+            mate_copy(i).wait_recv()
+            acc_ref[i] = (part + from_mate[i].astype(F32)).astype(jnp.bfloat16)
+            final_copy(block, piece, pair).start()
 
         return 0
 
-    lax.fori_loop(0, (n_tp - 1) * pieces, chain_step, 0)
+    lax.fori_loop(0, n_tp * pieces, pair_step, 0)
+
+    for piece in range(pieces):
+        i = z * pieces + piece
+        acc_own[piece] = product(i)
 
     for piece in range(pieces):
         i = z * pieces + piece
         cols = slice(piece * width, (piece + 1) * width)
-        total = product(i)
-        acc_ref[i] = total.astype(jnp.bfloat16)
-
-        @pl.when(z > 0)
-        def _():
-            right_copy(i).wait_recv()
-
-        @pl.when(z < n_tp - 1)
-        def _():
-            left_copy(i).wait_recv()
-
-        @pl.when(z == 0)
-        def _():
-            out_ref[:, cols] = (total + from_right[i].astype(F32)).astype(jnp.bfloat16)
-
-        @pl.when(z == n_tp - 1)
-        def _():
-            out_ref[:, cols] = (total + from_left[i].astype(F32)).astype(jnp.bfloat16)
-
-        @pl.when(jnp.logical_and(z > 0, z < n_tp - 1))
-        def _():
-            out_ref[:, cols] = (
-                total + from_left[i].astype(F32) + from_right[i].astype(F32)
-            ).astype(jnp.bfloat16)
+        for off in range(1, n_tp // 2):
+            sender = lax.rem(pair + off, n_tp // 2)
+            final_copy(z, piece, sender).wait_recv()
+            acc_own[piece] += final_in[sender * pieces + piece].astype(F32)
+        mate_copy(i).wait_recv()
+        out_ref[:, cols] = (acc_own[piece] + from_mate[i].astype(F32)).astype(jnp.bfloat16)
 
     @pl.when(me < n_seq - 1)
     def _():
@@ -315,15 +314,10 @@
 
     def drain(step, _):
         block, piece = step // pieces, step % pieces
-        i = block * pieces + piece
-
-        @pl.when(block > z)
+
+        @pl.when(block != z)
         def _():
-            right_copy(i).wait_send()
-
-        @pl.when(block < z)
-        def _():
-            left_copy(i).wait_send()
+            mate_copy(block * pieces + piece).wait_send()
 
         return 0
 
@@ -341,14 +335,18 @@
     width = min(256, block)
     pieces = block // width
     total = n_tp * pieces
-    vmem = pl.BlockSpec(memory_space=pltpu.VMEM)
     dma = pltpu.SemaphoreType.DMA
     return pl.pallas_call(
         functools.partial(kernel, n_seq, n_tp, pieces),
         out_shape=jax.ShapeDtypeStruct((rows, block), jnp.bfloat16),
-        in_specs=[vmem] * 7 + [pl.BlockSpec(memory_space=pl.ANY)],
-        out_specs=vmem,
+        in_specs=[pl.BlockSpec(memory_space=pltpu.HBM)] * 8,
+        out_specs=pl.BlockSpec(memory_space=pltpu.VMEM),
         scratch_shapes=[
+            pltpu.VMEM((3, rows, chans), jnp.bfloat16),
+            pltpu.VMEM(taps.shape, F32),
+            pltpu.VMEM((modes, groups), F32),
+            pltpu.VMEM((modes, groups), F32),
+            pltpu.VMEM((1, chans), F32),
             pltpu.VMEM((total, chans, width), jnp.bfloat16),
             pltpu.VMEM((3, rows + 8, chans), F32),
             pltpu.VMEM((rows, chans), F32),
@@ -367,16 +365,18 @@
             pltpu.VMEM((rows, chans), jnp.bfloat16),
             pltpu.VMEM((total, rows, width), jnp.bfloat16),
             pltpu.VMEM((total, rows, width), jnp.bfloat16),
-            pltpu.VMEM((total, rows, width), jnp.bfloat16),
+            pltpu.VMEM((n_tp // 2 * pieces, rows, width), jnp.bfloat16),
+            pltpu.VMEM((pieces, rows, width), F32),
+            dma((7,)),
             dma((total,)),
             dma((2,)),
             dma((n_seq,)), dma((n_seq,)), dma((n_seq,)), dma((n_seq,)),
-            dma((total,)), dma((total,)), dma((total,)), dma((total,)),
+            dma((total,)), dma((total,)), dma((n_tp // 2 * pieces,)),
         ],
         compiler_params=pltpu.CompilerParams(
-            collective_id=0, has_side_effects=True, vmem_limit_bytes=48 * 1024 * 1024
+            collective_id=0, has_side_effects=True, vmem_limit_bytes=63 * 1024 * 1024
         ),
-    )(q, k, v, taps, rates, res, skip.reshape(1, chans), w)
+    )(q, k, v, taps, rates.T, res.T, skip.reshape(1, chans), w)
 
 
 def solution(mesh):

time: 59.3 us -> 37.5 us (0.63)
  Pallas kernels: 52.4 us -> 35.7 us
  local copies, waits for them, and re-layouts: 6.52 us -> 1.67 us
    pallas_call x1, Pallas kernels: 52.4 us -> 35.7 us  [body(): pl.pallas_call(functools.partial(kernel, n_seq, n_tp, pieces), out_shape=...]
    unnamed x13 -> x1, local copies, waits for them, and re-layouts: 6.52 us -> 1.67 us
where the time goes in v1:
time: 37.5 us; the launch traced here: 37.4 us
  Pallas kernels  35.7 us (95%)
  local copies, waits for them, and re-layouts  1.67 us (4%)
    pallas_call x1, Pallas kernels, body(): pl.pallas_call(functools.partial(kernel, n_seq, n_tp, pieces), out_shape=...  35.7 us
    unnamed x1, local copies, waits for them, and re-layouts  1.67 us

profile of v1, /device:TPU:0, one launch (start us, length us, event | category | flops | bytes accessed | tf_op | source)
XLA Modules:
  0.0 37.4 jit_solution(18396827850540951426)
XLA Ops:
  0.0 35.7 %shard_map.82 = bf16[128,1024]{1,0:T(8,128)(2,1)} custom-call(bf16[128,1024]{1,0:T(8,128)(2,1)} %q_hbm.1, bf16[128,1024]{1,0:T(8,128)(2,1)} %k_hbm.1, bf16[128,1024]{1,0:T(8,128)(2,1)} %v_hbm.1, f32[3,1024]{1,0:T(4,128)} %taps_hbm.1, f32[16,64]{1,0:T(8,128)} %bitcast.3, f32[16,64]{1,0:T(8,128)} %bitcast.4, f32[1,1024]{1,0:T(1,128)} %bitcast.5, ...), custom_call_target="tpu_custom_call" | custom-call | tf_op jit(solution)/shard_map/pallas_call | solution.py:339
  35.7 1.7 %copy.10 = bf16[128,1024]{1,0:T(8,128)(2,1)} copy(bf16[128,1024]{1,0:T(8,128)(2,1)} %shard_map.82) | data formatting | bytes 524288

commit v2 on v1

--- a/solution.py
+++ b/solution.py
@@ -17,7 +17,7 @@
     q_hbm, k_hbm, v_hbm, taps_hbm, rates_hbm, res_hbm, skip_hbm, w_hbm,
     out_ref,
     qkv_ref, taps_ref, rates_ref, res_ref, skip_ref, w_vmem,
-    ext_ref, qf_ref, x3_ref, y3_ref, a3_ref, ar3_ref, r3_ref, s3_ref,
+    ext_ref, qf_ref, x3_ref, y3_ref, a3_ref, am3_ref, ar3_ref, r3_ref, s3_ref,
     halo_out, halo_in, state_ref, gathered, carries, carry_in, gated_ref,
     acc_ref, from_mate, final_in, acc_own,
     in_sem, w_sem, halo_sem, st_send, st_recv, ca_send, ca_recv,
@@ -71,21 +71,6 @@
     for load in loads:
         load.start()
 
-    pl.semaphore_wait(barrier, n_seq - 1 + n_tp - 1)
-
-    halo_copy = pltpu.make_async_remote_copy(
-        src_ref=halo_out,
-        dst_ref=halo_in,
-        send_sem=halo_sem.at[0],
-        recv_sem=halo_sem.at[1],
-        device_id={"seq": lax.rem(me + 1, n_seq)},
-        device_id_type=MESH,
-    )
-
-    @pl.when(me < n_seq - 1)
-    def _():
-        halo_copy.start()
-
     chan_id = lax.broadcasted_iota(jnp.int32, (groups, chans), 1)
     group_id = lax.broadcasted_iota(jnp.int32, (groups, chans), 0)
     onehot = (chan_id // group_size == group_id).astype(F32)
@@ -100,12 +85,57 @@
         cols = slice(s * LANES, (s + 1) * LANES)
         rate = rate_nat[:, cols]
         a3_ref[:, s, :] = jnp.exp(-rate)
+        am3_ref[:, s, :] = jnp.exp(-rate * float(rows - 2))
         ar3_ref[:, s, :] = jnp.exp(-rate * float(rows))
         r3_ref[:, s, :] = res_nat[:, cols]
         s3_ref[s : s + 1, :] = skip_ref[0:1, cols]
 
     for b in range(3):
+        ext_ref[b, 0:8, :] = jnp.zeros((8, chans), F32)
         ext_ref[b, 8 : 8 + rows, :] = qkv_ref[b].astype(F32)
+
+    pl.semaphore_wait(barrier, n_seq - 1 + n_tp - 1)
+
+    halo_copy = pltpu.make_async_remote_copy(
+        src_ref=halo_out,
+        dst_ref=halo_in,
+        send_sem=halo_sem.at[0],
+        recv_sem=halo_sem.at[1],
+        device_id={"seq": lax.rem(me + 1, n_seq)},
+        device_id_type=MESH,
+    )
+
+    @pl.when(me < n_seq - 1)
+    def _():
+        halo_copy.start()
+
+    def feature(b, cols, count):
+        return (
+            taps_ref[0:1, cols] * ext_ref[b, 8 : 8 + count, cols]
+            + taps_ref[1:2, cols] * ext_ref[b, 7 : 7 + count, cols]
+            + taps_ref[2:3, cols] * ext_ref[b, 6 : 6 + count, cols]
+        )
+
+
+    for s in range(subs):
+        cols = slice(s * LANES, (s + 1) * LANES)
+        x3_ref[:, s, :] = feature(1, cols, rows) * feature(2, cols, rows)
+
+    decays = [a3_ref[r] for r in range(modes)]
+
+    def state_step(t, hs):
+        x = x3_ref[t]
+        return tuple(decays[r] * hs[r] + x for r in range(modes))
+
+    zero = jnp.zeros((subs, LANES), F32)
+    hs = state_step(3, state_step(2, (zero,) * modes))
+    hs = lax.fori_loop(4, rows, state_step, hs, unroll=4)
+    for r in range(modes):
+        state_ref[r] = hs[r]
+
+    for s in range(subs):
+        cols = slice(s * LANES, (s + 1) * LANES)
+        qf_ref[:, cols] = feature(0, cols, rows)
 
     @pl.when(me == 0)
     def _():
@@ -118,27 +148,13 @@
     for b in range(3):
         ext_ref[b, 6:8, :] = halo_in[2 * b : 2 * b + 2, :]
 
-    def feature(b, cols):
-        return (
-            taps_ref[0:1, cols] * ext_ref[b, 8 : 8 + rows, cols]
-            + taps_ref[1:2, cols] * ext_ref[b, 7 : 7 + rows, cols]
-            + taps_ref[2:3, cols] * ext_ref[b, 6 : 6 + rows, cols]
-        )
-
     for s in range(subs):
         cols = slice(s * LANES, (s + 1) * LANES)
-        x3_ref[:, s, :] = feature(1, cols) * feature(2, cols)
-
-    decays = [a3_ref[r] for r in range(modes)]
-
-    def state_step(t, hs):
-        x = x3_ref[t]
-        return tuple(decays[r] * hs[r] + x for r in range(modes))
-
-    zero = jnp.zeros((subs, LANES), F32)
-    hs = lax.fori_loop(0, rows, state_step, (zero,) * modes, unroll=4)
+        x3_ref[0:8, s, :] = feature(1, cols, 8) * feature(2, cols, 8)
+        qf_ref[0:8, cols] = feature(0, cols, 8)
+    first, second = x3_ref[0], x3_ref[1]
     for r in range(modes):
-        state_ref[r] = hs[r]
+        state_ref[r] += am3_ref[r] * (second + a3_ref[r] * first)
 
     def state_copy(off):
         to = lax.rem(me + off, n_seq)
@@ -170,11 +186,7 @@
 
     for off in range(1, n_seq):
         copy, to = state_copy(off)
-        when_owner(to, copy.start)
-
-    for s in range(subs):
-        cols = slice(s * LANES, (s + 1) * LANES)
-        qf_ref[:, cols] = feature(0, cols)
+        pl.when(jnp.logical_and(to < owners, me < n_seq - 1))(copy.start)
 
     weights = [r3_ref[r] for r in range(modes)]
     skip = s3_ref[...]
@@ -190,26 +202,35 @@
         y3_ref[t] = y
         return tuple(out)
 
-    lax.fori_loop(0, rows, local_step, (zero,) * modes, unroll=2)
+    half = rows // 2
+    hs = lax.fori_loop(0, half, local_step, (zero,) * modes, unroll=2)
 
     def own_modes():
         mine = pl.ds(me * per_owner, per_owner)
         gathered[me] = state_ref[mine]
         for off in range(1, n_seq):
-            state_copy(off)[0].wait_recv()
+            sender = lax.rem(me - off + n_seq, n_seq)
+            pl.when(sender < n_seq - 1)(state_copy(off)[0].wait_recv)
         block_decay = ar3_ref[mine]
         carry = jnp.zeros((per_owner, subs, LANES), F32)
         for j in range(n_seq):
             carries[j] = carry
-            carry = block_decay * carry + gathered[j]
+            if j < n_seq - 1:
+                carry = block_decay * carry + gathered[j]
         for off in range(1, n_seq):
-            carry_copy(off)[0].start()
+            copy, to = carry_copy(off)
+            pl.when(to > 0)(copy.start)
         carry_in[mine] = carries[me]
 
     when_owner(me, own_modes)
+    lax.fori_loop(half, rows, local_step, hs, unroll=2)
     for off in range(1, n_seq):
         sender = lax.rem(me - off + n_seq, n_seq)
-        when_owner(sender, carry_copy(off)[0].wait_recv)
+        pl.when(jnp.logical_and(sender < owners, me > 0))(carry_copy(off)[0].wait_recv)
+
+    @pl.when(me == 0)
+    def _():
+        carry_in[...] = jnp.zeros_like(carry_in)
 
     def carry_step(t, gs):
         y = y3_ref[t]
@@ -309,8 +330,8 @@
 
     for off in range(1, n_seq):
         copy, to = state_copy(off)
-        when_owner(to, copy.wait_send)
-        when_owner(me, carry_copy(off)[0].wait_send)
+        pl.when(jnp.logical_and(to < owners, me < n_seq - 1))(copy.wait_send)
+        pl.when(jnp.logical_and(me < owners, to > 0))(carry_copy(off)[0].wait_send)
 
     def drain(step, _):
         block, piece = step // pieces, step % pieces
@@ -355,6 +376,7 @@
             pltpu.VMEM((modes, subs, LANES), F32),
             pltpu.VMEM((modes, subs, LANES), F32),
             pltpu.VMEM((modes, subs, LANES), F32),
+            pltpu.VMEM((modes, subs, LANES), F32),
             pltpu.VMEM((subs, LANES), F32),
             pltpu.VMEM((8, chans), F32),
             pltpu.VMEM((8, chans), F32),

time: 37.5 us -> 35.7 us (0.952)
  the two profiles are of different devices: /device:TPU:0 before, /device:TPU:12 now
where the time goes in v2:
time: 35.7 us; the launch traced here: 35.5 us
  Pallas kernels  33.8 us (95%)
  local copies, waits for them, and re-layouts  1.67 us (5%)
    pallas_call x1, Pallas kernels, body(): pl.pallas_call(functools.partial(kernel, n_seq, n_tp, pieces), out_shape=...  33.8 us
    unnamed x1, local copies, waits for them, and re-layouts  1.67 us

profile of v2, /device:TPU:12, one launch (start us, length us, event | category | flops | bytes accessed | tf_op | source)
XLA Modules:
  0.0 35.5 jit_solution(3750317564297812923)
XLA Ops:
  0.0 33.8 %shard_map.82 = bf16[128,1024]{1,0:T(8,128)(2,1)} custom-call(bf16[128,1024]{1,0:T(8,128)(2,1)} %q_hbm.1, bf16[128,1024]{1,0:T(8,128)(2,1)} %k_hbm.1, bf16[128,1024]{1,0:T(8,128)(2,1)} %v_hbm.1, f32[3,1024]{1,0:T(4,128)} %taps_hbm.1, f32[16,64]{1,0:T(8,128)} %bitcast.3, f32[16,64]{1,0:T(8,128)} %bitcast.4, f32[1,1024]{1,0:T(1,128)} %bitcast.5, ...), custom_call_target="tpu_custom_call" | custom-call | tf_op jit(solution)/shard_map/pallas_call | solution.py:360
  33.9 1.7 %copy.10 = bf16[128,1024]{1,0:T(8,128)(2,1)} copy(bf16[128,1024]{1,0:T(8,128)(2,1)} %shard_map.82) | data formatting | bytes 524288
